TPU v7x, 32 devices: a whole 2x2x4 slice. The times are simulated.
32 devices in a mesh: scen: 8 (over z, y), blk: 4 (over x, core).
Axes of the slice: x: 2, y: 2, z: 4, core: 2. Of those that a mesh axis runs over, the one named last changes fastest.
Arguments:
- draws: bfloat16 [2048, 8192], P('blk', 'scen'), may hold values from -6 to 6
- factor: bfloat16 [8192, 8192], P('scen', 'blk'), may hold values from -0.1875 to 0.1875
- occupancy: int32 [16, 16], replicated, may hold values from 0 to 1, as said below
Outputs:
- scenarios: bfloat16 [2048, 8192], P('blk', 'scen')
Inputs may be any that keep to these rules, and one draw needn't show every extreme that they name: occupancy[i, i] is 1 for every i, occupancy[i, j] is 0 for j > i, and each entry below the diagonal is 0 or 1.
All inputs are finite; a program needn't handle non-finite values.
Results may differ from a plain program's by a relative error of at most 0.001.
Values may be sent and summed in bfloat16 or wider, within the bound.
A program may use at most 64 MiB of HBM per device.

v0:
```python
import jax
import jax.numpy as jnp
from jax import lax
from jax.sharding import PartitionSpec as P

TILE = 512


def keep_mask(row_start, row_count, col_count, occ_float):
    tile_ids = jnp.arange(occ_float.shape[0], dtype=jnp.int32)
    rows = row_start + jnp.arange(row_count, dtype=jnp.int32)
    cols = jnp.arange(col_count, dtype=jnp.int32)
    row_hot = (rows[:, None] // TILE == tile_ids[None, :]).astype(jnp.float32)
    col_hot = (cols[:, None] // TILE == tile_ids[None, :]).astype(jnp.float32)
    occ_rows = jnp.dot(row_hot, occ_float)
    marked = jnp.dot(occ_rows, col_hot.T) > 0.5
    return marked & (cols[None, :] <= rows[:, None])


def times_transposed(left, right):
    return lax.dot_general(
        left, right, (((1,), (1,)), ((), ())), preferred_element_type=jnp.float32
    )


def local(draws, factor, occupancy):
    rows_own = factor.shape[0]
    row_start = lax.axis_index("scen") * rows_own
    occ_float = occupancy.astype(jnp.float32)
    zero_value = jnp.zeros((), factor.dtype)
    whole = lax.all_gather(draws, "scen", axis=1, tiled=True)
    piece = lax.all_gather(factor, "blk", axis=1, tiled=True)
    count = piece.shape[1]
    keep = keep_mask(row_start, rows_own, count, occ_float)
    used = jnp.where(keep, piece, zero_value)
    result = times_transposed(whole, used)
    return result.astype(jnp.bfloat16)


def solution(mesh):
    return jax.shard_map(
        local,
        mesh=mesh,
        in_specs=(P("blk", "scen"), P("scen", "blk"), P()),
        out_specs=P("blk", "scen"),
        check_vma=False,
    )
```

profile of v0, /device:TPU:26, one launch (start us, length us, event | category | flops | bytes accessed | tf_op | source)
XLA Modules:
  0.0 270.5 jit_solution(5792998088914908058)
XLA Ops:
  6.5 0.0 all-gather.5.cloned.1.call-start
  6.5 0.7 all-gather.5.cloned.1.call-update
  7.3 0.0 all-gather.3.cloned.1.call-start
  7.3 0.7 all-gather.3.cloned.1.call-update
  8.0 1.0 fusion.13
  9.1 124.5 %all-gather.5.cloned.1.call-done = bf16[512,8192]{1,0:T(8,128)(2,1)} async-done(((bf16[512,1024]{1,0:T(8,128)(2,1)}), bf16[512,8192]{1,0:T(8,128)(2,1)}) %all-gather.5.cloned.1.call-update) | async-done | bytes 8388624 | tf_op jit(solution)/shard_map/all_gather | solution.py:31
  133.5 106.7 %all-gather.3.cloned.1.call-done = bf16[1024,8192]{1,0:T(8,128)(2,1)} async-done(((bf16[1024,2048]{1,0:T(8,128)(2,1)}), bf16[1024,8192]{1,0:T(8,128)(2,1)}) %all-gather.3.cloned.1.call-update) | async-done | bytes 16777232 | tf_op jit(solution)/shard_map/all_gather | solution.py:32
  240.2 22.1 %fusion.10 = bf16[512,1024]{0,1:T(8,128)(2,1)S(1)} fusion(bf16[512,8192]{1,0:T(8,128)(2,1)} %all-gather.5.cloned.1.call-done, bf16[1024,8192]{1,0:T(8,128)(2,1)} %all-gather.3.cloned.1.call-done, s32[1024]{0:T(1024)S(1)} %get-tuple-element.6, bf16[1024,16]{1,0:T(8,128)(2,1)S(1)} %fusion.13, s32[8192]{0:T(1024)S(1)} %add_select_fusion), kind=kOutput, calls=%fused_computation.7 | convolution fusion | flops 8892579840 | bytes 26284032 | tf_op jit(solution)/shard_map/dot_general | solution.py:21
  262.3 1.3 copy.5
  (2 shorter events, 0.0 us)
Async XLA Ops:
  6.5 127.0 %all-gather.5.cloned.1.call-start = ((), (), s32[]{:S(2)}) async-start(), calls=%async_computation.1 | async-start | bytes 9437184 | tf_op jit(solution)/shard_map/all_gather | solution.py:31
  7.3 233.0 %all-gather.3.cloned.1.call-start = ((), (), s32[]{:S(2)}) async-start(), calls=%async_computation | async-start | bytes 20971520 | tf_op jit(solution)/shard_map/all_gather | solution.py:32
Sparse Core Ops, SparseCore 0:
  9.5 123.9 all-gather.4
  135.1 105.1 all-gather.2
where the time goes:
time: 273 us; the launch traced here: 270 us
  waiting for transfers between devices  233 us (85%)
  matrix products  23.1 us (8%)
  between operations  13.4 us (5%)
    all_gather x1, waiting for transfers between devices, local(): whole = lax.all_gather(draws, 'scen', axis=1, tiled=True)  124 us
    all_gather x1, waiting for transfers between devices, local(): piece = lax.all_gather(factor, 'blk', axis=1, tiled=True)  107 us
    dot_general x1, matrix products, times_transposed(): lax.dot_general(left, right, (((1,), (1,)), ((), ())), preferred_element_...  22.1 us
  transfers between devices with their start and end apart: 2, of which 2 were waited for; matrix products, arithmetic and copies ran while one was open for 0% of the time, Pallas kernels for 0%

commit v1 on v0

v1 whole, which is shorter than its diff:
```python
import functools

import jax
import jax.numpy as jnp
from jax import lax
from jax.experimental import pallas as pl
from jax.experimental.pallas import tpu as pltpu
from jax.sharding import PartitionSpec as P

MESH = pl.DeviceIdType.MESH


def kernel(
    tile, scens, blks,
    draws, factor, occ, out,
    dbuf, fbuf, acc,
    zsend, zrecv, ysend, yrecv, xsend, xrecv, csend, crecv, dload, fload,
):
    levels, groups = scens // 2, blks // 2
    rows, cols = factor.shape
    rt_n, ct_n = rows // tile, cols // tile
    half = draws.shape[0] // 2
    z_n = levels * rt_n
    f_n = rt_n * ct_n
    x_n = (groups - 1) * f_n
    k = lax.axis_index("scen")
    b = lax.axis_index("blk")
    z, y = k // 2, k % 2
    x, c = b // 2, b % 2

    def d_tile(n, col):
        return ((z - n // rt_n) * 2 + col) * rt_n + n % rt_n

    def d_has(n, col):
        lev = z - n // rt_n
        return (n >= 0) & (n < z_n) & (lev >= 0) & (lev * 2 + col <= k)

    def when(inside, cond, body):
        if inside:
            pl.when(cond())(body)

    def z_copy(n, recv):
        t = d_tile(n, y)
        i = n if recv else n + rt_n
        return pltpu.make_async_remote_copy(
            src_ref=dbuf.at[t], dst_ref=dbuf.at[t],
            send_sem=zsend.at[n], recv_sem=zrecv.at[i],
            device_id=(k + 2, b), device_id_type=MESH,
        )

    def y_copy(n, recv):
        t = d_tile(n, 1 - y if recv else y)
        return pltpu.make_async_remote_copy(
            src_ref=dbuf.at[t], dst_ref=dbuf.at[t],
            send_sem=ysend.at[n], recv_sem=yrecv.at[n],
            device_id=(z * 2 + 1 - y, b), device_id_type=MESH,
        )

    def y_sends(n):
        return d_has(n, y) & ((y == 0) | (n >= rt_n))

    def f_at(owner, f):
        return owner * ct_n + (ct_n - 1 - f // rt_n), f % rt_n

    def f_has(owner, f):
        t, r = f_at(owner, f)
        return t <= k * rt_n + r

    def x_owner(m, sending):
        step = m // f_n + 1
        other = lax.rem(x + step, groups) if sending else lax.rem(x + groups - step, groups)
        return other * 2 + c

    def x_copy(m, sending):
        f = m % f_n
        peer = x_owner(m, sending)
        t, r = f_at(b if sending else peer, f)
        return pltpu.make_async_remote_copy(
            src_ref=fbuf.at[t, r], dst_ref=fbuf.at[t, r],
            send_sem=xsend.at[m], recv_sem=xrecv.at[m],
            device_id=(k, peer), device_id_type=MESH,
        )

    def x_has(m, sending):
        return (m >= 0) & (m < x_n) & f_has(b if sending else x_owner(m, sending), m % f_n)

    def c_owner(q, core):
        m = q - f_n
        step = m // f_n + 1
        other = lax.rem(x + groups - step, groups)
        return jnp.where(q < f_n, x, other) * 2 + core

    def c_copy(q, core):
        t, r = f_at(c_owner(q, core), q % f_n)
        return pltpu.make_async_remote_copy(
            src_ref=fbuf.at[t, r], dst_ref=fbuf.at[t, r],
            send_sem=csend.at[q], recv_sem=crecv.at[q],
            device_id=(k, x * 2 + 1 - c), device_id_type=MESH,
        )

    def c_has(q, core):
        return (q >= 0) & (q < f_n + x_n) & f_has(c_owner(q, core), q % f_n)

    def d_load(h):
        return pltpu.make_async_copy(
            draws.at[:, pl.ds(h * tile, tile)], dbuf.at[k * rt_n + h], dload.at[h]
        )

    def f_load(f):
        t, r = f_at(b, f)
        lt = ct_n - 1 - f // rt_n
        return pltpu.make_async_copy(
            factor.at[pl.ds(r * tile, tile), pl.ds(lt * tile, tile)],
            fbuf.at[t, r],
            fload.at[f],
        )

    for h in range(rt_n):
        d_load(h).start()

    def load_f(f):
        @pl.when(f_has(b, f))
        def _():
            f_load(f).start()

    for f in range(f_n):
        load_f(f)

    barrier = pltpu.get_barrier_semaphore()

    def greet(kk, bb):
        pl.semaphore_signal(barrier, inc=1, device_id=(kk, bb), device_id_type=MESH)

    greet(z * 2 + 1 - y, b)
    greet(k, x * 2 + 1 - c)
    for step in range(1, groups):
        greet(k, lax.rem(x + step, groups) * 2 + c)

    @pl.when(z > 0)
    def _():
        greet(k - 2, b)

    @pl.when(z < levels - 1)
    def _():
        greet(k + 2, b)

    ends = jnp.where(z > 0, 1, 0) + jnp.where(z < levels - 1, 1, 0)
    pl.semaphore_wait(barrier, groups + 1 + ends)

    def forward_d(n):
        if n + rt_n < z_n:
            pl.when(z < levels - 1)(lambda: z_copy(n, False).start())
        pl.when(y_sends(n))(lambda: y_copy(n, False).start())

    def send_x(m):
        when(0 <= m < x_n, lambda: x_has(m, True), lambda: x_copy(m, True).start())

    for h in range(rt_n):
        d_load(h).wait()
        forward_d(h)

    def wait_f(f):
        @pl.when(f_has(b, f))
        def _():
            f_load(f).wait()

    for f in range(f_n):
        wait_f(f)
    send_x(0)
    send_x(1)

    def give_own(q):
        pl.when(c_has(q, c))(lambda: c_copy(q, c).start())

    for q in range(f_n):
        give_own(q)

    acc[...] = jnp.zeros_like(acc)

    def d_tick(t):
        owner, h = t // rt_n, t % rt_n
        lev, col = owner // 2, owner % 2
        n = (z - lev) * rt_n + h
        same = jnp.where(lev == z, 0, n - rt_n + 1)
        return jnp.where(col == y, same, n + 1)

    def f_tick(t, r):
        owner = t // ct_n
        f = (ct_n - 1 - t % ct_n) * rt_n + r
        ox, oc = owner // 2, owner % 2
        m = (lax.rem(x - ox + groups, groups) - 1) * f_n + f
        near = jnp.where(oc == c, 0, 1)
        far = jnp.where(oc == c, m + 1, m + 2)
        return jnp.where(ox == x, near, far)

    def product(t, r, masked):
        block = fbuf[t, r]
        if masked:
            row = lax.broadcasted_iota(jnp.int32, block.shape, 0)
            col = lax.broadcasted_iota(jnp.int32, block.shape, 1)
            block = jnp.where(col <= row, block.astype(jnp.float32), 0.0).astype(block.dtype)
        at_row = lax.broadcasted_iota(jnp.int32, occ.shape, 0) == k * rt_n + r
        at_col = lax.broadcasted_iota(jnp.int32, occ.shape, 1) == t
        mark = jnp.where(at_row & at_col, occ[...].astype(jnp.float32), 0.0)
        on = jnp.sum(jnp.sum(mark, axis=1, keepdims=True), axis=0, keepdims=True)
        for s in range(0, draws.shape[0], half):
            part = lax.dot_general(
                dbuf[t, s:s + half], block, (((1,), (1,)), ((), ())),
                preferred_element_type=jnp.float32,
            )
            acc[r, s:s + half] += part * on

    def compute(now):
        def one(t, carry):
            for r in range(rt_n):
                top = k * rt_n + r
                due = (t <= top) & (jnp.maximum(d_tick(t), f_tick(t, r)) == now)
                pl.when(due & (t < top))(lambda r=r: product(t, r, False))
                pl.when(due & (t == top))(lambda r=r: product(t, r, True))
            return carry

        lax.fori_loop(0, scens * rt_n, one, 0)

    def take(q):
        when(0 <= q < f_n + x_n, lambda: c_has(q, 1 - c), lambda: c_copy(q, 1 - c).wait_recv())

    def tick(now):
        n, m = now + rt_n - 1, now - 1

        def d_arrived():
            z_copy(n, True).wait_recv()
            forward_d(n)

        def x_arrived():
            x_copy(m, False).wait_recv()
            c_copy(m + f_n, c).start()

        when(now >= 1 and n < z_n, lambda: d_has(n, y), d_arrived)
        when(0 <= m < x_n, lambda: x_has(m, False), x_arrived)
        when(0 <= m < x_n, lambda: x_has(m, True), lambda: x_copy(m, True).wait_send())
        if now >= 1:
            send_x(now + 1)
        when(
            0 <= m < z_n, lambda: d_has(m, 1 - y), lambda: y_copy(m, True).wait_recv()
        )
        if now == 1:
            for q in range(f_n):
                take(q)
        if now >= 2:
            take(f_n + now - 2)
        compute(now)

    for now in range(max(z_n + 1, x_n + 2, 2)):
        tick(now)

    for r in range(rt_n):
        out[:, r * tile:(r + 1) * tile] = acc[r].astype(out.dtype)

    def drain_d(n):
        if n + rt_n < z_n:
            pl.when(d_has(n, y) & (z < levels - 1))(lambda: z_copy(n, False).wait_send())
        pl.when(y_sends(n))(lambda: y_copy(n, False).wait_send())

    for n in range(z_n):
        drain_d(n)

    def drain_c(q):
        pl.when(c_has(q, c))(lambda: c_copy(q, c).wait_send())

    for q in range(f_n + x_n):
        drain_c(q)


def local(scens, blks, draws, factor, occupancy):
    count, rows = draws.shape
    cols = factor.shape[1]
    tile = rows * scens // occupancy.shape[0]
    tiles = occupancy.shape[0]
    rt_n, ct_n = rows // tile, cols // tile
    z_n, f_n = scens // 2 * rt_n, rt_n * ct_n
    x_n = (blks // 2 - 1) * f_n
    dma = pltpu.SemaphoreType.DMA
    return pl.pallas_call(
        functools.partial(kernel, tile, scens, blks),
        out_shape=jax.ShapeDtypeStruct((count, rows), jnp.bfloat16),
        in_specs=[
            pl.BlockSpec(memory_space=pltpu.HBM),
            pl.BlockSpec(memory_space=pltpu.HBM),
            pl.BlockSpec(memory_space=pltpu.VMEM),
        ],
        out_specs=pl.BlockSpec(memory_space=pltpu.VMEM),
        scratch_shapes=[
            pltpu.VMEM((tiles, count, tile), jnp.bfloat16),
            pltpu.VMEM((tiles, rt_n, tile, tile), jnp.bfloat16),
            pltpu.VMEM((rt_n, count, tile), jnp.float32),
            dma((z_n,)), dma((z_n,)), dma((z_n,)), dma((z_n,)),
            dma((x_n,)), dma((x_n,)), dma((f_n + x_n,)), dma((f_n + x_n,)),
            dma((rt_n,)), dma((f_n,)),
        ],
        compiler_params=pltpu.CompilerParams(
            collective_id=0, has_side_effects=True, vmem_limit_bytes=48 * 1024 * 1024
        ),
        cost_estimate=pl.CostEstimate(
            flops=count * rows * rows * scens, bytes_accessed=8 * 1024 * 1024, transcendentals=0
        ),
    )(draws, factor, occupancy)


def solution(mesh):
    return jax.shard_map(
        functools.partial(local, mesh.shape["scen"], mesh.shape["blk"]),
        mesh=mesh,
        in_specs=(P("blk", "scen"), P("scen", "blk"), P()),
        out_specs=P("blk", "scen"),
        check_vma=False,
    )
```

time: 273 us -> 102 us (0.37)
  waiting for transfers between devices: 233 us -> 0 us
  Pallas kernels: 0 us -> 99 us
  matrix products: 23.1 us -> 0 us
  between operations: 13.4 us -> 0.01 us
    all_gather x2 -> x0, waiting for transfers between devices: 231 us -> none  [the longest x1 124 us: local(): whole = lax.all_gather(draws, 'scen', axis=1, tiled=True)]
    pallas_call x0 -> x1, Pallas kernels: none -> 99 us  [local(): pl.pallas_call(functools.partial(kernel, tile, scens, blks), out_shape=ja...]
    dot_general x2 -> x0, matrix products: 23.1 us -> none  [the longest x1 22.1 us: times_transposed(): lax.dot_general(left, right, (((1,), (1,)), ((), ())), preferred_element_...]
    unnamed x0 -> x5, local copies, waits for them, and re-layouts: none -> 2.89 us
  transfers between devices with their start and end apart: 2 -> 0, of which waited for: 2 -> 0; matrix products, arithmetic and copies ran while one was open for 0% -> 0% of each run, Pallas kernels for 0% -> 0%
where the time goes in v1:
time: 102 us
  Pallas kernels  99 us (97%)
  local copies, waits for them, and re-layouts  2.89 us (3%)
    pallas_call x1, Pallas kernels, local(): pl.pallas_call(functools.partial(kernel, tile, scens, blks), out_shape=ja...  99 us
    unnamed x5, local copies, waits for them, and re-layouts  2.89 us

profile of v1, /device:TPU:26, one launch (start us, length us, event | category | flops | bytes accessed | tf_op | source)
XLA Modules:
  0.0 101.9 jit_solution(14418925246971317680)
XLA Ops:
  0.0 0.0 copy-start
  0.0 1.2 %copy-done = bf16[512,1024]{1,0:T(8,128)(2,1)S(1)} copy-done((bf16[512,1024]{1,0:T(8,128)(2,1)S(1)}, bf16[512,1024]{1,0:T(8,128)(2,1)}, u32[]{:S(2)}) %copy-start) | copy-done | bytes 1048600
  1.2 0.0 copy-start.1
  1.2 0.7 copy-done.1
  1.9 99.0 %shard_map.37 = bf16[512,1024]{1,0:T(8,128)(2,1)S(1)} custom-call(bf16[512,1024]{1,0:T(8,128)(2,1)S(1)} %copy-done, bf16[1024,2048]{1,0:T(8,128)(2,1)} %factor.1, s32[16,16]{1,0:T(8,128)S(1)} %copy-done.1), custom_call_target="tpu_custom_call" | custom-call | flops 4294967296 | bytes 8388608 | tf_op jit(solution)/shard_map/pallas_call | solution.py:283
  100.9 1.0 copy.5
Async XLA Ops:
  0.0 1.2 %copy-start = (bf16[512,1024]{1,0:T(8,128)(2,1)S(1)}, bf16[512,1024]{1,0:T(8,128)(2,1)}, u32[]{:S(2)}) copy-start(bf16[512,1024]{1,0:T(8,128)(2,1)} %draws.1) | copy-start | bytes 3145732
  1.2 0.7 copy-start.1

commit v2 on v1

--- a/solution.py
+++ b/solution.py
@@ -14,7 +14,7 @@
     tile, scens, blks,
     draws, factor, occ, out,
     dbuf, fbuf, acc,
-    zsend, zrecv, ysend, yrecv, xsend, xrecv, csend, crecv, dload, fload,
+    zsend, zrecv, ysend, yrecv, xsend, xrecv, csend, crecv, esend, erecv, dload, fload,
 ):
     levels, groups = scens // 2, blks // 2
     rows, cols = factor.shape
@@ -56,8 +56,24 @@
             device_id=(z * 2 + 1 - y, b), device_id_type=MESH,
         )
 
+    early = rt_n > 1 and levels > 1
+
+    def y_has(n, col):
+        has = d_has(n, col)
+        if early and n % rt_n == rt_n - 1:
+            has &= (col == 1) | (z == 0) | (n // rt_n != z)
+        return has
+
     def y_sends(n):
-        return d_has(n, y) & ((y == 0) | (n >= rt_n))
+        return y_has(n, y) & ((y == 0) | (n >= rt_n))
+
+    def e_copy():
+        t = rt_n - 1
+        return pltpu.make_async_remote_copy(
+            src_ref=dbuf.at[t], dst_ref=dbuf.at[t],
+            send_sem=esend.at[0], recv_sem=erecv.at[0],
+            device_id=(k + 2, b), device_id_type=MESH,
+        )
 
     def f_at(owner, f):
         return owner * ct_n + (ct_n - 1 - f // rt_n), f % rt_n
@@ -166,8 +182,10 @@
 
     for f in range(f_n):
         wait_f(f)
-    send_x(0)
-    send_x(1)
+        if f < 2:
+            send_x(f)
+    for m in range(f_n, 2):
+        send_x(m)
 
     def give_own(q):
         pl.when(c_has(q, c))(lambda: c_copy(q, c).start())
@@ -182,7 +200,10 @@
         lev, col = owner // 2, owner % 2
         n = (z - lev) * rt_n + h
         same = jnp.where(lev == z, 0, n - rt_n + 1)
-        return jnp.where(col == y, same, n + 1)
+        due = jnp.where(col == y, same, n + 1)
+        if early:
+            due = jnp.where((t == rt_n - 1) & (y == 1) & (z > 0), z * rt_n + 1, due)
+        return due
 
     def f_tick(t, r):
         owner = t // ct_n
@@ -231,6 +252,10 @@
             z_copy(n, True).wait_recv()
             forward_d(n)
 
+        def e_arrived():
+            e_copy().wait_recv()
+            pl.when(z < levels - 1)(lambda: e_copy().start())
+
         def x_arrived():
             x_copy(m, False).wait_recv()
             c_copy(m + f_n, c).start()
@@ -240,9 +265,13 @@
         when(0 <= m < x_n, lambda: x_has(m, True), lambda: x_copy(m, True).wait_send())
         if now >= 1:
             send_x(now + 1)
+        if early:
+            pl.when((y == 1) & (z > 0) & (z * rt_n + 1 == now))(e_arrived)
         when(
-            0 <= m < z_n, lambda: d_has(m, 1 - y), lambda: y_copy(m, True).wait_recv()
-        )
+            0 <= m < z_n, lambda: y_has(m, 1 - y), lambda: y_copy(m, True).wait_recv()
+        )
+        if early and m == rt_n - 1:
+            pl.when((y == 1) & (z == 0))(lambda: e_copy().start())
         if now == 1:
             for q in range(f_n):
                 take(q)
@@ -263,6 +292,9 @@
 
     for n in range(z_n):
         drain_d(n)
+
+    if early:
+        pl.when((y == 1) & (z < levels - 1))(lambda: e_copy().wait_send())
 
     def drain_c(q):
         pl.when(c_has(q, c))(lambda: c_copy(q, c).wait_send())
@@ -295,7 +327,7 @@
             pltpu.VMEM((rt_n, count, tile), jnp.float32),
             dma((z_n,)), dma((z_n,)), dma((z_n,)), dma((z_n,)),
             dma((x_n,)), dma((x_n,)), dma((f_n + x_n,)), dma((f_n + x_n,)),
-            dma((rt_n,)), dma((f_n,)),
+            dma((1,)), dma((1,)), dma((rt_n,)), dma((f_n,)),
         ],
         compiler_params=pltpu.CompilerParams(
             collective_id=0, has_side_effects=True, vmem_limit_bytes=48 * 1024 * 1024

time: 102 us -> 101 us (level)
  no operation moved by 1% of the time
where the time goes in v2:
time: 101 us
  Pallas kernels  98.2 us (97%)
  local copies, waits for them, and re-layouts  2.89 us (3%)
    pallas_call x1, Pallas kernels, local(): pl.pallas_call(functools.partial(kernel, tile, scens, blks), out_shape=ja...  98.2 us
    unnamed x5, local copies, waits for them, and re-layouts  2.89 us

profile of v2, /device:TPU:26, one launch (start us, length us, event | category | flops | bytes accessed | tf_op | source)
XLA Modules:
  0.0 101.1 jit_solution(18015220169472820282)
XLA Ops:
  0.0 0.0 copy-start
  0.0 1.2 %copy-done = bf16[512,1024]{1,0:T(8,128)(2,1)S(1)} copy-done((bf16[512,1024]{1,0:T(8,128)(2,1)S(1)}, bf16[512,1024]{1,0:T(8,128)(2,1)}, u32[]{:S(2)}) %copy-start) | copy-done | bytes 1048600
  1.2 0.0 copy-start.1
  1.2 0.7 copy-done.1
  1.9 98.2 %shard_map.37 = bf16[512,1024]{1,0:T(8,128)(2,1)S(1)} custom-call(bf16[512,1024]{1,0:T(8,128)(2,1)S(1)} %copy-done, bf16[1024,2048]{1,0:T(8,128)(2,1)} %factor.1, s32[16,16]{1,0:T(8,128)S(1)} %copy-done.1), custom_call_target="tpu_custom_call" | custom-call | flops 4294967296 | bytes 8388608 | tf_op jit(solution)/shard_map/pallas_call | solution.py:315
  100.1 1.0 copy.5
Async XLA Ops:
  0.0 1.2 %copy-start = (bf16[512,1024]{1,0:T(8,128)(2,1)S(1)}, bf16[512,1024]{1,0:T(8,128)(2,1)}, u32[]{:S(2)}) copy-start(bf16[512,1024]{1,0:T(8,128)(2,1)} %draws.1) | copy-start | bytes 3145732
  1.2 0.7 copy-start.1
